TPU v7x, 256 devices: a whole 4x4x8 slice. The times are simulated.
256 devices in a mesh: seq: 32 (over z_lo, x, y), head: 8 (over z_hi, core).
Axes of the slice: x: 4, y: 4, z: 8 (z_hi: 4, z_lo: 2; z = z_hi * 2 + z_lo), core: 2. Of those that a mesh axis runs over, the one named last changes fastest.
Arguments:
- query_tokens: bfloat16 [40960, 3072], P(('seq', 'head')), may hold values from -6 to 6
- key_tokens: bfloat16 [40960, 3072], P(('seq', 'head')), may hold values from -6 to 6
- value_tokens: bfloat16 [40960, 3072], P(('seq', 'head')), may hold values from -6 to 6
- matching: int32 [2, 32], replicated, may hold values from 0 to 31, as said below
Outputs:
- attended: bfloat16 [40960, 3072], P(('seq', 'head'))
Inputs may be any that keep to these rules, and one draw needn't show every extreme that they name: For each round r and block b: matching[r, matching[r, b]] == b and matching[r, b] != b; the 2 rows give every block different partners.
All inputs are finite; a program needn't handle non-finite values.
Results may differ from a plain program's by a relative error of at most 0.0048.
Values may be sent and summed in bfloat16 or wider, within the bound.
A program may use at most 64 MiB of HBM per device.

v0:
```python
import math
import jax
import jax.numpy as jnp
from jax import lax
from jax.sharding import PartitionSpec as P

HEAD_DIM = 128
ROUNDS = 2


def attend(query_rows, key_rows, value_rows, head_size):
    row_count, feature_width = query_rows.shape
    heads_here = feature_width // head_size
    block_rows = math.gcd(row_count, 512)
    score_scale = 1.0 / math.sqrt(head_size)
    key_heads = key_rows.reshape(-1, heads_here, head_size)
    value_heads = value_rows.reshape(-1, heads_here, head_size)
    query_blocks = query_rows.reshape(row_count // block_rows, block_rows, heads_here, head_size)

    def one_block(query_block):
        scores = (
            jnp.einsum("qhd,khd->hqk", query_block, key_heads, preferred_element_type=jnp.float32)
            * score_scale
        )
        weights = jnp.exp(scores - jnp.max(scores, axis=-1, keepdims=True))
        totals = jnp.sum(weights, axis=-1)
        mixed = jnp.einsum(
            "hqk,khd->qhd",
            weights.astype(jnp.bfloat16),
            value_heads,
            preferred_element_type=jnp.float32,
        )
        return (mixed / jnp.transpose(totals)[:, :, None]).astype(jnp.bfloat16)

    return lax.map(one_block, query_blocks).reshape(row_count, feature_width)


def per_device(query_tokens, key_tokens, value_tokens, matching):
    seq_count = lax.axis_size("seq")
    local_query, local_keys, local_values = (
        lax.all_to_all(query_tokens, "head", split_axis=1, concat_axis=0, tiled=True),
        lax.all_to_all(key_tokens, "head", split_axis=1, concat_axis=0, tiled=True),
        lax.all_to_all(value_tokens, "head", split_axis=1, concat_axis=0, tiled=True),
    )
    block_count, feature_width = local_keys.shape
    piece_rows = block_count // seq_count
    spread_keys, spread_values = (
        lax.all_to_all(
            local_keys.reshape(seq_count, piece_rows, feature_width),
            "seq",
            split_axis=0,
            concat_axis=0,
            tiled=True,
        ),
        lax.all_to_all(
            local_values.reshape(seq_count, piece_rows, feature_width),
            "seq",
            split_axis=0,
            concat_axis=0,
            tiled=True,
        ),
    )
    key_parts = []
    value_parts = []
    for round_index in range(ROUNDS):
        got_keys, got_values = (
            lax.all_to_all(
                jnp.take(spread_keys, matching[round_index], axis=0),
                "seq",
                split_axis=0,
                concat_axis=0,
                tiled=True,
            ),
            lax.all_to_all(
                jnp.take(spread_values, matching[round_index], axis=0),
                "seq",
                split_axis=0,
                concat_axis=0,
                tiled=True,
            ),
        )
        key_parts.append(got_keys.reshape(block_count, feature_width))
        value_parts.append(got_values.reshape(block_count, feature_width))
    partner_keys = jnp.concatenate(key_parts, 0)
    partner_values = jnp.concatenate(value_parts, 0)
    key_rows = jnp.concatenate([local_keys, partner_keys], 0)
    value_rows = jnp.concatenate([local_values, partner_values], 0)
    attended = attend(local_query, key_rows, value_rows, HEAD_DIM)
    return lax.all_to_all(attended, "head", split_axis=0, concat_axis=1, tiled=True)


def solution(mesh):
    return jax.shard_map(
        per_device,
        mesh=mesh,
        in_specs=(
            P(("seq", "head"), None),
            P(("seq", "head"), None),
            P(("seq", "head"), None),
            P(),
        ),
        out_specs=P(("seq", "head"), None),
        check_vma=False,
    )
```

profile of v0, /device:TPU:2, one launch (start us, length us, event | category | flops | bytes accessed | tf_op | source)
XLA Modules:
  0.0 343.2 jit_solution(16645471671025664687)
XLA Ops:
  0.0 0.0 copy-start.2
  0.0 2.3 copy.36
  2.3 8.5 %all-to-all-start.1 = ((bf16[160,8,384]{2,0,1:T(8,128)(2,1)}), bf16[160,8,384]{2,0,1:T(8,128)(2,1)S(1)}, u32[]{:S(2)}, u32[]{:S(2)}) async-start(bf16[160,8,384]{2,0,1:T(8,128)(2,1)} %bitcast.48), calls=%async_computation.1 | async-start | bytes 1966080 | tf_op jit(solution)/shard_map/all_to_all | solution.py:42
  10.8 0.0 copy-done.2
  10.8 0.1 copy.35
  10.9 27.8 %all-to-all-done.1 = bf16[160,8,384]{2,0,1:T(8,128)(2,1)S(1)} async-done(((bf16[160,8,384]{2,0,1:T(8,128)(2,1)}), bf16[160,8,384]{2,0,1:T(8,128)(2,1)S(1)}, u32[]{:S(2)}, u32[]{:S(2)}) %all-to-all-start.1) | async-done | bytes 983072 | tf_op jit(solution)/shard_map/all_to_all | solution.py:42
  38.7 31.0 %all_to_all.97 = bf16[160,8,384]{2,0,1:T(8,128)(2,1)} all-to-all(bf16[160,8,384]{2,0,1:T(8,128)(2,1)S(1)} %bitcast.65), channel_id=1, replica_groups=mesh['seq'=32,'head'=8] {'head'}, dimensions={1} | all-to-all | bytes 1966080 | tf_op jit(solution)/shard_map/all_to_all | solution.py:43
  69.7 21.4 %all_to_all.98 = bf16[32,40,384]{2,1,0:T(8,128)(2,1)S(1)} all-to-all(bf16[32,40,384]{2,1,0:T(8,128)(2,1)S(1)} %bitcast.62), channel_id=1, replica_groups=mesh['seq'=32,'head'=8] {'seq'}, dimensions={0} | all-to-all | bytes 1966080 | tf_op jit(solution)/shard_map/all_to_all | solution.py:48
  91.1 5.6 %all-to-all-start.6 = ((bf16[32,40,384]{2,1,0:T(8,128)(2,1)}), bf16[32,40,384]{2,1,0:T(8,128)(2,1)S(1)}, u32[]{:S(2)}, u32[]{:S(2)}) async-start(bf16[32,40,384]{2,1,0:T(8,128)(2,1)} %bitcast.10), calls=%async_computation.6 | async-start | bytes 1966080 | tf_op jit(solution)/shard_map/all_to_all | solution.py:55
  96.7 2.2 copy.37
  99.0 10.1 %all-to-all-done.6 = bf16[32,40,384]{2,1,0:T(8,128)(2,1)S(1)} async-done(((bf16[32,40,384]{2,1,0:T(8,128)(2,1)}), bf16[32,40,384]{2,1,0:T(8,128)(2,1)S(1)}, u32[]{:S(2)}, u32[]{:S(2)}) %all-to-all-start.6) | async-done | bytes 983072 | tf_op jit(solution)/shard_map/all_to_all | solution.py:55
  109.1 4.6 %all-to-all-start = ((bf16[160,8,384]{2,0,1:T(8,128)(2,1)}), bf16[160,8,384]{2,0,1:T(8,128)(2,1)}, u32[]{:S(2)}, u32[]{:S(2)}) async-start(bf16[160,8,384]{2,0,1:T(8,128)(2,1)} %bitcast.64), calls=%async_computation | async-start | bytes 1966080 | tf_op jit(solution)/shard_map/all_to_all | solution.py:41
  113.7 0.0 copy-done.3
  113.7 1.6 gather_fusion
  115.4 1.7 gather_fusion.2
  117.0 3.1 broadcast_select_fusion.2
  120.1 21.9 %all-to-all-done = bf16[160,8,384]{2,0,1:T(8,128)(2,1)} async-done(((bf16[160,8,384]{2,0,1:T(8,128)(2,1)}), bf16[160,8,384]{2,0,1:T(8,128)(2,1)}, u32[]{:S(2)}, u32[]{:S(2)}) %all-to-all-start) | async-done | bytes 983072 | tf_op jit(solution)/shard_map/all_to_all | solution.py:41
  142.0 5.3 %all-to-all-start.3 = ((bf16[32,40,384]{2,1,0:T(8,128)(2,1)}), bf16[32,40,384]{2,1,0:T(8,128)(2,1)}, u32[]{:S(2)}, u32[]{:S(2)}) async-start(bf16[32,40,384]{2,1,0:T(8,128)(2,1)} %get-tuple-element.68), calls=%async_computation.3 | async-start | bytes 1966080 | tf_op jit(solution)/shard_map/all_to_all | solution.py:67
  147.3 1.7 gather_fusion.1
  149.0 1.6 gather_fusion.3
  150.6 2.8 broadcast_select_fusion
  153.4 8.9 %all-to-all-done.3 = bf16[32,40,384]{2,1,0:T(8,128)(2,1)} async-done(((bf16[32,40,384]{2,1,0:T(8,128)(2,1)}), bf16[32,40,384]{2,1,0:T(8,128)(2,1)}, u32[]{:S(2)}, u32[]{:S(2)}) %all-to-all-start.3) | async-done | bytes 983072 | tf_op jit(solution)/shard_map/all_to_all | solution.py:67
  162.3 19.4 %all_to_all.99 = bf16[32,40,384]{2,1,0:T(8,128)(2,1)} all-to-all(bf16[32,40,384]{2,1,0:T(8,128)(2,1)S(1)} %get-tuple-element.70), channel_id=1, replica_groups=mesh['seq'=32,'head'=8] {'seq'}, dimensions={0} | all-to-all | bytes 1966080 | tf_op jit(solution)/shard_map/all_to_all | solution.py:67
  181.7 0.0 copy-done
  181.7 18.4 %all_to_all.100 = bf16[32,40,384]{2,1,0:T(8,128)(2,1)} all-to-all(bf16[32,40,384]{2,1,0:T(8,128)(2,1)S(1)} %copy-done), channel_id=1, replica_groups=mesh['seq'=32,'head'=8] {'seq'}, dimensions={0} | all-to-all | bytes 1966080 | tf_op jit(solution)/shard_map/all_to_all | solution.py:74
  200.1 5.8 %all-to-all-start.8 = ((bf16[32,40,384]{2,1,0:T(8,128)(2,1)}), bf16[32,40,384]{2,1,0:T(8,128)(2,1)}, u32[]{:S(2)}, u32[]{:S(2)}) async-start(bf16[32,40,384]{2,1,0:T(8,128)(2,1)} %get-tuple-element.69), calls=%async_computation.8 | async-start | bytes 1966080 | tf_op jit(solution)/shard_map/all_to_all | solution.py:74
  206.0 0.3 concatenate.20
  206.3 3.7 %concatenate.24 = bf16[1280,3,128]{2,1,0:T(4,128)(2,1)} reshape(bf16[8,160,384]{2,1,0:T(8,128)(2,1)} %bitcast.9) | data formatting | bytes 1966080 | tf_op jit(solution)/shard_map/concatenate | solution.py:87
  210.0 2.6 reshape.51
  212.7 1.2 copy.23
  213.8 2.6 concatenate.21
  216.5 3.7 %concatenate.22 = bf16[1280,3,128]{2,1,0:T(4,128)(2,1)} reshape(bf16[32,40,384]{2,1,0:T(8,128)(2,1)} %all_to_all.99) | data formatting | bytes 1966080 | tf_op jit(solution)/shard_map/concatenate | solution.py:86
  220.2 26.4 %pad_maximum_fusion = bf16[3840,3,128]{2,1,0:T(4,128)(2,1)S(1)} fusion(bf16[1280,3,128]{2,1,0:T(4,128)(2,1)} %concatenate.22, bf16[1280,3,128]{2,1,0:T(4,128)(2,1)S(1)} %concatenate.21, bf16[1280,3,128]{2,1,0:T(4,128)(2,1)S(1)} %concatenate.20), kind=kLoop, calls=%fused_computation.21 | loop fusion | flops 2949120 | bytes 5898240 | tf_op jit(solution)/shard_map/concatenate | solution.py:86
  246.6 0.4 copy.24
  247.1 3.7 %concatenate.25 = bf16[1280,3,128]{2,1,0:T(4,128)(2,1)} reshape(bf16[32,40,384]{2,1,0:T(8,128)(2,1)} %all_to_all.100) | data formatting | bytes 1966080 | tf_op jit(solution)/shard_map/concatenate | solution.py:87
  250.7 0.0 all-to-all-done.8
  250.7 3.7 %concatenate.26 = bf16[1280,3,128]{2,1,0:T(4,128)(2,1)} reshape(bf16[32,40,384]{2,1,0:T(8,128)(2,1)} %all-to-all-done.8) | data formatting | bytes 1966080 | tf_op jit(solution)/shard_map/concatenate | solution.py:87
  254.4 11.2 %pad_maximum_fusion.1 = bf16[3840,3,128]{2,1,0:T(4,128)(2,1)S(1)} fusion(bf16[1280,3,128]{2,1,0:T(4,128)(2,1)} %concatenate.26, bf16[1280,3,128]{2,1,0:T(4,128)(2,1)} %concatenate.25, bf16[1280,3,128]{2,1,0:T(4,128)(2,1)} %concatenate.24), kind=kLoop, calls=%fused_computation.22 | loop fusion | flops 2949120 | bytes 5898240 | tf_op jit(solution)/shard_map/concatenate | solution.py:87
  265.6 2.0 copy.25
  267.6 40.9 %while.10 = (s32[]{:T(128)}, bf16[5,256,3,128]{3,1,2,0:T(8,128)(2,1)}, bf16[5,256,3,128]{3,1,2,0:T(8,128)(2,1)}, bf16[3840,3,128]{2,0,1:T(8,128)(2,1)S(1)}, bf16[3840,3,128]{2,0,1:T(8,128)(2,1)}, /*index=5*/s32[]{:T(128)}) while((s32[]{:T(128)}, bf16[5,256,3,128]{3,1,2,0:T(8,128)(2,1)}, bf16[5,256,3,128]{3,1,2,0:T(8,128)(2,1)}, ...), condition=%wide.region_3.5_spmd, body=%wide.region_0.4_spmd.sunk | while | flops 1533737472 | bytes 53493856 | solution.py:35
  267.6 2.7 multiply_reduce_fusion.2
  270.3 2.1 fusion.36
  272.4 0.0 copy-done.1
  272.4 3.4 fusion.37
  275.8 2.7 multiply_reduce_fusion.2
  278.5 2.1 fusion.36
  280.6 0.0 copy-done.1
  280.6 3.4 fusion.37
  284.0 2.7 multiply_reduce_fusion.2
  286.7 2.1 fusion.36
  288.7 0.0 copy-done.1
  288.7 3.4 fusion.37
  292.2 2.7 multiply_reduce_fusion.2
  294.9 2.1 fusion.36
  296.9 0.0 copy-done.1
  296.9 3.4 fusion.37
  300.3 2.7 multiply_reduce_fusion.2
  303.1 2.1 fusion.36
  305.1 0.0 copy-done.1
  305.1 3.4 fusion.37
  308.5 2.0 copy.26
  310.6 0.9 all_to_all.83
  311.4 30.6 %all_to_all.101 = bf16[8,160,384]{2,1,0:T(8,128)(2,1)S(1)} all-to-all(bf16[8,160,384]{2,1,0:T(8,128)(2,1)S(1)} %all_to_all.83), channel_id=1, replica_groups=mesh['seq'=32,'head'=8] {'head'}, dimensions={0} | all-to-all | bytes 1966080 | tf_op jit(solution)/shard_map/all_to_all | solution.py:89
  342.1 1.1 copy.31
  (11 shorter events, 0.0 us)
Async XLA Ops:
  0.0 10.8 %copy-start.2 = (bf16[160,3072]{1,0:T(8,128)(2,1)S(1)}, bf16[160,3072]{1,0:T(8,128)(2,1)}, u32[]{:S(2)}) copy-start(bf16[160,3072]{1,0:T(8,128)(2,1)} %param.10) | copy-start | bytes 2949124
  2.3 36.4 %all-to-all-start.1 = ((bf16[160,8,384]{2,0,1:T(8,128)(2,1)}), bf16[160,8,384]{2,0,1:T(8,128)(2,1)S(1)}, u32[]{:S(2)}, u32[]{:S(2)}) async-start(bf16[160,8,384]{2,0,1:T(8,128)(2,1)} %bitcast.48), calls=%async_computation.1 | async-start | bytes 1966080 | tf_op jit(solution)/shard_map/all_to_all | solution.py:42
  69.7 44.0 %copy-start.3 = (s32[2,32]{1,0:T(2,128)S(1)}, s32[2,32]{1,0:T(2,128)}, u32[]{:S(2)}) copy-start(s32[2,32]{1,0:T(2,128)} %param.11) | copy-start | bytes 772
  91.1 18.0 %all-to-all-start.6 = ((bf16[32,40,384]{2,1,0:T(8,128)(2,1)}), bf16[32,40,384]{2,1,0:T(8,128)(2,1)S(1)}, u32[]{:S(2)}, u32[]{:S(2)}) async-start(bf16[32,40,384]{2,1,0:T(8,128)(2,1)} %bitcast.10), calls=%async_computation.6 | async-start | bytes 1966080 | tf_op jit(solution)/shard_map/all_to_all | solution.py:55
  109.1 32.9 %all-to-all-start = ((bf16[160,8,384]{2,0,1:T(8,128)(2,1)}), bf16[160,8,384]{2,0,1:T(8,128)(2,1)}, u32[]{:S(2)}, u32[]{:S(2)}) async-start(bf16[160,8,384]{2,0,1:T(8,128)(2,1)} %bitcast.64), calls=%async_computation | async-start | bytes 1966080 | tf_op jit(solution)/shard_map/all_to_all | solution.py:41
  142.0 20.3 %all-to-all-start.3 = ((bf16[32,40,384]{2,1,0:T(8,128)(2,1)}), bf16[32,40,384]{2,1,0:T(8,128)(2,1)}, u32[]{:S(2)}, u32[]{:S(2)}) async-start(bf16[32,40,384]{2,1,0:T(8,128)(2,1)} %get-tuple-element.68), calls=%async_computation.3 | async-start | bytes 1966080 | tf_op jit(solution)/shard_map/all_to_all | solution.py:67
  149.0 32.7 %copy-start = (bf16[32,40,384]{2,1,0:T(8,128)(2,1)S(1)}, bf16[32,40,384]{2,1,0:T(8,128)(2,1)}, u32[]{:S(2)}) copy-start(bf16[32,40,384]{2,1,0:T(8,128)(2,1)} %get-tuple-element.67) | copy-start | bytes 2949124
  200.1 50.6 %all-to-all-start.8 = ((bf16[32,40,384]{2,1,0:T(8,128)(2,1)}), bf16[32,40,384]{2,1,0:T(8,128)(2,1)}, u32[]{:S(2)}, u32[]{:S(2)}) async-start(bf16[32,40,384]{2,1,0:T(8,128)(2,1)} %get-tuple-element.69), calls=%async_computation.8 | async-start | bytes 1966080 | tf_op jit(solution)/shard_map/all_to_all | solution.py:74
  270.3 2.1 copy-start.1
  278.5 2.1 copy-start.1
  286.7 2.1 copy-start.1
  294.9 2.1 copy-start.1
  303.0 2.1 copy-start.1
where the time goes:
time: 345 us; the launch traced here: 343 us
  blocking collectives  121 us (35%)
  waiting for transfers between devices  68.7 us (20%)
  other arithmetic  53.7 us (16%)
  local copies, waits for them, and re-layouts  39.4 us (11%)
  matrix products  30.6 us (9%)
  starting transfers between devices  29.8 us (9%)
    all_to_all x1, blocking collectives, per_device(): lax.all_to_all(value_tokens, 'head', split_axis=1, concat_axis=0, tiled=T...  31 us
    all_to_all x1, blocking collectives, per_device(): lax.all_to_all(attended, 'head', split_axis=0, concat_axis=1, tiled=True)  30.6 us
    all_to_all x1, waiting for transfers between devices, per_device(): lax.all_to_all(key_tokens, 'head', split_axis=1, concat_axis=0, tiled=True)  27.8 us
    concatenate x1, other arithmetic, per_device(): key_rows = jnp.concatenate([local_keys, partner_keys], 0)  26.4 us
    all_to_all x1, waiting for transfers between devices, per_device(): lax.all_to_all(query_tokens, 'head', split_axis=1, concat_axis=0, tiled=T...  21.9 us
    all_to_all x1, blocking collectives, per_device(): lax.all_to_all(local_keys.reshape(seq_count, piece_rows, feature_width),...  21.4 us
    all_to_all x1, blocking collectives, per_device(): lax.all_to_all(jnp.take(spread_keys, matching[round_index], axis=0), 'seq...  19.4 us
    all_to_all x1, blocking collectives, per_device(): lax.all_to_all(jnp.take(spread_values, matching[round_index], axis=0), 's...  18.4 us
  transfers between devices with their start and end apart: 5, of which 4 were waited for; matrix products, arithmetic and copies ran while one was open for 17% of the time, Pallas kernels for 0%

commit v1 on v0

--- a/solution.py
+++ b/solution.py
@@ -40,7 +40,12 @@
     local_query, local_keys, local_values = (
         lax.all_to_all(query_tokens, "head", split_axis=1, concat_axis=0, tiled=True),
         lax.all_to_all(key_tokens, "head", split_axis=1, concat_axis=0, tiled=True),
-        lax.all_to_all(value_tokens, "head", split_axis=1, concat_axis=0, tiled=True),
+        jnp.concatenate(
+            lax.all_to_all(
+                jnp.stack(jnp.split(value_tokens, lax.axis_size("head"), axis=1)), "head", 0, 0
+            ),
+            axis=0,
+        ),
     )
     block_count, feature_width = local_keys.shape
     piece_rows = block_count // seq_count

time: 345 us -> 358 us (1.038)
  local copies, waits for them, and re-layouts: 39.4 us -> 47.2 us
  other arithmetic: 53.7 us -> 59.2 us
    unnamed x6 -> x15, local copies, waits for them, and re-layouts: 0.01 us -> 11 us
    all_to_all x1, waiting for transfers between devices: 8.88 us -> 0.01 us  [per_device(): lax.all_to_all(jnp.take(spread_keys, matching[round_index], axis=0), 'seq...]
    all_to_all x1, waiting for transfers between devices: 0.01 us -> 8.47 us  [per_device(): lax.all_to_all(jnp.take(spread_values, matching[round_index], axis=0), 's...]
    concatenate x3, local copies, waits for them, and re-layouts: 11.1 us -> 5.19 us  [per_device(): value_rows = jnp.concatenate([local_values, partner_values], 0)]
    concatenate x1, other arithmetic: 11.2 us -> 16.3 us  [per_device(): value_rows = jnp.concatenate([local_values, partner_values], 0)]
  transfers between devices with their start and end apart: 5 -> 5, of which waited for: 4 -> 4; matrix products, arithmetic and copies ran while one was open for 17% -> 14% of each run, Pallas kernels for 0% -> 0%
where the time goes in v1:
time: 358 us; the launch traced here: 357 us
  blocking collectives  121 us (34%)
  waiting for transfers between devices  68.3 us (19%)
  other arithmetic  59.2 us (17%)
  local copies, waits for them, and re-layouts  47.2 us (13%)
  matrix products  30.6 us (9%)
  starting transfers between devices  29.8 us (8%)
    all_to_all x1, blocking collectives, per_device(): lax.all_to_all(key_tokens, 'head', split_axis=1, concat_axis=0, tiled=True)  31 us
    all_to_all x1, blocking collectives, per_device(): lax.all_to_all(attended, 'head', split_axis=0, concat_axis=1, tiled=True)  30.6 us
    all_to_all x1, waiting for transfers between devices, per_device(): lax.all_to_all(jnp.stack(jnp.split(value_tokens, lax.axis_size('head'), a...  27.8 us
    concatenate x1, other arithmetic, per_device(): key_rows = jnp.concatenate([local_keys, partner_keys], 0)  26.4 us
    all_to_all x1, waiting for transfers between devices, per_device(): lax.all_to_all(query_tokens, 'head', split_axis=1, concat_axis=0, tiled=T...  21.9 us
    all_to_all x1, blocking collectives, per_device(): lax.all_to_all(local_values.reshape(seq_count, piece_rows, feature_width)...  21.4 us
    all_to_all x1, blocking collectives, per_device(): lax.all_to_all(jnp.take(spread_values, matching[round_index], axis=0), 's...  19.5 us
    all_to_all x1, blocking collectives, per_device(): lax.all_to_all(jnp.take(spread_keys, matching[round_index], axis=0), 'seq...  18.4 us
  transfers between devices with their start and end apart: 5, of which 4 were waited for; matrix products, arithmetic and copies ran while one was open for 14% of the time, Pallas kernels for 0%

profile of v1, /device:TPU:2, one launch (start us, length us, event | category | flops | bytes accessed | tf_op | source)
XLA Modules:
  0.0 356.6 jit_solution(10639120948624782407)
XLA Ops:
  0.0 1.6 bitcast_dynamic-update-slice_fusion.7
  1.6 1.6 bitcast_dynamic-update-slice_fusion.6
  3.2 1.6 bitcast_dynamic-update-slice_fusion.5
  4.8 1.6 bitcast_dynamic-update-slice_fusion.4
  6.3 1.6 bitcast_dynamic-update-slice_fusion.3
  7.9 1.6 bitcast_dynamic-update-slice_fusion.2
  9.5 1.6 bitcast_dynamic-update-slice_fusion.1
  11.0 1.6 bitcast_dynamic-update-slice_fusion
  12.6 8.5 %all-to-all-start.5 = ((bf16[8,160,384]{2,1,0:T(8,128)(2,1)}), bf16[8,160,384]{2,1,0:T(8,128)(2,1)S(1)}, u32[]{:S(2)}, u32[]{:S(2)}) async-start(bf16[8,160,384]{2,1,0:T(8,128)(2,1)} %bitcast_dynamic-update-slice_fusion), calls=%async_computation.5 | async-start | bytes 1966080 | tf_op jit(solution)/shard_map/all_to_all | solution.py:44
  21.1 0.1 copy.30
  21.2 27.8 %all-to-all-done.5 = bf16[8,160,384]{2,1,0:T(8,128)(2,1)S(1)} async-done(((bf16[8,160,384]{2,1,0:T(8,128)(2,1)}), bf16[8,160,384]{2,1,0:T(8,128)(2,1)S(1)}, u32[]{:S(2)}, u32[]{:S(2)}) %all-to-all-start.5) | async-done | bytes 983072 | tf_op jit(solution)/shard_map/all_to_all | solution.py:44
  48.9 31.0 %all_to_all.86 = bf16[160,8,384]{2,0,1:T(8,128)(2,1)} all-to-all(bf16[160,8,384]{2,0,1:T(8,128)(2,1)S(1)} %bitcast.74), channel_id=1, replica_groups=mesh['seq'=32,'head'=8] {'head'}, dimensions={1} | all-to-all | bytes 1966080 | tf_op jit(solution)/shard_map/all_to_all | solution.py:42
  79.9 21.4 %all_to_all.87 = bf16[32,40,384]{2,1,0:T(8,128)(2,1)S(1)} all-to-all(bf16[32,40,384]{2,1,0:T(8,128)(2,1)S(1)} %bitcast.72), channel_id=1, replica_groups=mesh['seq'=32,'head'=8] {'seq'}, dimensions={0} | all-to-all | bytes 1966080 | tf_op jit(solution)/shard_map/all_to_all | solution.py:60
  101.3 5.6 %all-to-all-start.2 = ((bf16[32,40,384]{2,1,0:T(8,128)(2,1)}), bf16[32,40,384]{2,1,0:T(8,128)(2,1)S(1)}, u32[]{:S(2)}, u32[]{:S(2)}) async-start(bf16[32,40,384]{2,1,0:T(8,128)(2,1)} %bitcast.7), calls=%async_computation.2 | async-start | bytes 1966080 | tf_op jit(solution)/shard_map/all_to_all | solution.py:53
  107.0 2.2 copy.31
  109.2 10.1 %all-to-all-done.2 = bf16[32,40,384]{2,1,0:T(8,128)(2,1)S(1)} async-done(((bf16[32,40,384]{2,1,0:T(8,128)(2,1)}), bf16[32,40,384]{2,1,0:T(8,128)(2,1)S(1)}, u32[]{:S(2)}, u32[]{:S(2)}) %all-to-all-start.2) | async-done | bytes 983072 | tf_op jit(solution)/shard_map/all_to_all | solution.py:53
  119.3 4.6 %all-to-all-start = ((bf16[160,8,384]{2,0,1:T(8,128)(2,1)}), bf16[160,8,384]{2,0,1:T(8,128)(2,1)}, u32[]{:S(2)}, u32[]{:S(2)}) async-start(bf16[160,8,384]{2,0,1:T(8,128)(2,1)} %bitcast.73), calls=%async_computation | async-start | bytes 1966080 | tf_op jit(solution)/shard_map/all_to_all | solution.py:41
  124.0 1.6 gather_fusion.2
  125.6 1.6 gather_fusion
  127.3 3.1 broadcast_select_fusion.2
  130.4 21.9 %all-to-all-done = bf16[160,8,384]{2,0,1:T(8,128)(2,1)} async-done(((bf16[160,8,384]{2,0,1:T(8,128)(2,1)}), bf16[160,8,384]{2,0,1:T(8,128)(2,1)}, u32[]{:S(2)}, u32[]{:S(2)}) %all-to-all-start) | async-done | bytes 983072 | tf_op jit(solution)/shard_map/all_to_all | solution.py:41
  152.2 5.3 %all-to-all-start.7 = ((bf16[32,40,384]{2,1,0:T(8,128)(2,1)}), bf16[32,40,384]{2,1,0:T(8,128)(2,1)}, u32[]{:S(2)}, u32[]{:S(2)}) async-start(bf16[32,40,384]{2,1,0:T(8,128)(2,1)} %get-tuple-element.67), calls=%async_computation.7 | async-start | bytes 1966080 | tf_op jit(solution)/shard_map/all_to_all | solution.py:79
  157.6 1.6 gather_fusion.3
  159.2 1.7 gather_fusion.1
  160.9 3.1 broadcast_select_fusion
  164.1 8.5 %all-to-all-done.7 = bf16[32,40,384]{2,1,0:T(8,128)(2,1)} async-done(((bf16[32,40,384]{2,1,0:T(8,128)(2,1)}), bf16[32,40,384]{2,1,0:T(8,128)(2,1)}, u32[]{:S(2)}, u32[]{:S(2)}) %all-to-all-start.7) | async-done | bytes 983072 | tf_op jit(solution)/shard_map/all_to_all | solution.py:79
  172.5 19.5 %all_to_all.88 = bf16[32,40,384]{2,1,0:T(8,128)(2,1)S(1)} all-to-all(bf16[32,40,384]{2,1,0:T(8,128)(2,1)} %get-tuple-element.69), channel_id=1, replica_groups=mesh['seq'=32,'head'=8] {'seq'}, dimensions={0} | all-to-all | bytes 1966080 | tf_op jit(solution)/shard_map/all_to_all | solution.py:79
  192.1 18.4 %all_to_all.89 = bf16[32,40,384]{2,1,0:T(8,128)(2,1)} all-to-all(bf16[32,40,384]{2,1,0:T(8,128)(2,1)S(1)} %copy-done.1), channel_id=1, replica_groups=mesh['seq'=32,'head'=8] {'seq'}, dimensions={0} | all-to-all | bytes 1966080 | tf_op jit(solution)/shard_map/all_to_all | solution.py:72
  210.5 5.8 %all-to-all-start.4 = ((bf16[32,40,384]{2,1,0:T(8,128)(2,1)}), bf16[32,40,384]{2,1,0:T(8,128)(2,1)}, u32[]{:S(2)}, u32[]{:S(2)}) async-start(bf16[32,40,384]{2,1,0:T(8,128)(2,1)} %get-tuple-element.70), calls=%async_computation.4 | async-start | bytes 1966080 | tf_op jit(solution)/shard_map/all_to_all | solution.py:72
  216.3 3.7 %concatenate.20 = bf16[1280,3,128]{2,1,0:T(4,128)(2,1)} reshape(bf16[8,160,384]{2,1,0:T(8,128)(2,1)} %bitcast.5) | data formatting | bytes 1966080 | tf_op jit(solution)/shard_map/concatenate | solution.py:91
  220.0 2.6 reshape.45
  222.7 1.2 copy.20
  223.9 0.3 concatenate.24
  224.2 3.7 %concatenate.25 = bf16[1280,3,128]{2,1,0:T(4,128)(2,1)} reshape(bf16[32,40,384]{2,1,0:T(8,128)(2,1)} %all-to-all-done.7) | data formatting | bytes 1966080 | tf_op jit(solution)/shard_map/concatenate | solution.py:92
  227.9 1.2 concatenate.26
  229.0 16.3 %pad_maximum_fusion.1 = bf16[3840,3,128]{2,1,0:T(4,128)(2,1)S(1)} fusion(bf16[1280,3,128]{2,1,0:T(4,128)(2,1)} %concatenate.26, bf16[1280,3,128]{2,1,0:T(4,128)(2,1)} %concatenate.25, bf16[1280,3,128]{2,1,0:T(4,128)(2,1)S(1)} %concatenate.24), kind=kLoop, calls=%fused_computation.22 | loop fusion | flops 2949120 | bytes 5898240 | tf_op jit(solution)/shard_map/concatenate | solution.py:92
  245.4 2.0 copy.22
  247.4 2.7 concatenate.21
  250.2 0.0 all-to-all-done.4
  250.2 3.7 %concatenate.22 = bf16[1280,3,128]{2,1,0:T(4,128)(2,1)} reshape(bf16[32,40,384]{2,1,0:T(8,128)(2,1)} %all-to-all-done.4) | data formatting | bytes 1966080 | tf_op jit(solution)/shard_map/concatenate | solution.py:91
  253.9 26.4 %pad_maximum_fusion = bf16[3840,3,128]{2,1,0:T(4,128)(2,1)S(1)} fusion(bf16[1280,3,128]{2,1,0:T(4,128)(2,1)} %concatenate.22, bf16[1280,3,128]{2,1,0:T(4,128)(2,1)S(1)} %concatenate.21, bf16[1280,3,128]{2,1,0:T(4,128)(2,1)S(1)} %copy-done), kind=kLoop, calls=%fused_computation.21 | loop fusion | flops 2949120 | bytes 5898240 | tf_op jit(solution)/shard_map/concatenate | solution.py:91
  280.3 0.4 copy.21
  280.7 41.2 %while.10 = (s32[]{:T(128)}, bf16[5,256,3,128]{3,1,2,0:T(8,128)(2,1)}, bf16[5,256,3,128]{3,1,2,0:T(8,128)(2,1)}, bf16[3840,3,128]{2,0,1:T(8,128)(2,1)S(1)}, bf16[3840,3,128]{2,0,1:T(8,128)(2,1)}, /*index=5*/s32[]{:T(128)}) while((s32[]{:T(128)}, bf16[5,256,3,128]{3,1,2,0:T(8,128)(2,1)}, bf16[5,256,3,128]{3,1,2,0:T(8,128)(2,1)}, ...), condition=%wide.region_3.5_spmd, body=%wide.region_0.4_spmd.sunk | while | flops 1533737472 | bytes 53493856 | solution.py:35
  281.0 2.7 multiply_reduce_fusion.2
  283.7 2.1 fusion.36
  285.8 3.4 fusion.37
  289.2 2.7 multiply_reduce_fusion.2
  291.9 2.1 fusion.36
  294.0 3.4 fusion.37
  297.4 2.7 multiply_reduce_fusion.2
  300.1 2.1 fusion.36
  302.1 0.0 copy-done.2
  302.2 3.4 fusion.37
  305.6 2.7 multiply_reduce_fusion.2
  308.3 2.1 fusion.36
  310.3 0.0 copy-done.2
  310.3 3.4 fusion.37
  313.7 2.7 multiply_reduce_fusion.2
  316.5 2.1 fusion.36
  318.5 3.4 fusion.37
  321.9 2.0 copy.23
  324.0 0.9 all_to_all.72
  324.8 30.6 %all_to_all.90 = bf16[8,160,384]{2,1,0:T(8,128)(2,1)S(1)} all-to-all(bf16[8,160,384]{2,1,0:T(8,128)(2,1)S(1)} %all_to_all.72), channel_id=1, replica_groups=mesh['seq'=32,'head'=8] {'head'}, dimensions={0} | all-to-all | bytes 1966080 | tf_op jit(solution)/shard_map/all_to_all | solution.py:94
  355.5 1.1 copy.27
  (20 shorter events, 0.1 us)
Async XLA Ops:
  0.0 21.0 %copy-start.3 = (bf16[160,3072]{1,0:T(8,128)(2,1)S(1)}, bf16[160,3072]{1,0:T(8,128)(2,1)}, u32[]{:S(2)}) copy-start(bf16[160,3072]{1,0:T(8,128)(2,1)} %param.9) | copy-start | bytes 2949124
  12.6 36.4 %all-to-all-start.5 = ((bf16[8,160,384]{2,1,0:T(8,128)(2,1)}), bf16[8,160,384]{2,1,0:T(8,128)(2,1)S(1)}, u32[]{:S(2)}, u32[]{:S(2)}) async-start(bf16[8,160,384]{2,1,0:T(8,128)(2,1)} %bitcast_dynamic-update-slice_fusion), calls=%async_computation.5 | async-start | bytes 1966080 | tf_op jit(solution)/shard_map/all_to_all | solution.py:44
  79.9 44.0 %copy-start.4 = (s32[2,32]{1,0:T(2,128)S(1)}, s32[2,32]{1,0:T(2,128)}, u32[]{:S(2)}) copy-start(s32[2,32]{1,0:T(2,128)} %param.11) | copy-start | bytes 772
  101.3 18.0 %all-to-all-start.2 = ((bf16[32,40,384]{2,1,0:T(8,128)(2,1)}), bf16[32,40,384]{2,1,0:T(8,128)(2,1)S(1)}, u32[]{:S(2)}, u32[]{:S(2)}) async-start(bf16[32,40,384]{2,1,0:T(8,128)(2,1)} %bitcast.7), calls=%async_computation.2 | async-start | bytes 1966080 | tf_op jit(solution)/shard_map/all_to_all | solution.py:53
  119.3 32.9 %all-to-all-start = ((bf16[160,8,384]{2,0,1:T(8,128)(2,1)}), bf16[160,8,384]{2,0,1:T(8,128)(2,1)}, u32[]{:S(2)}, u32[]{:S(2)}) async-start(bf16[160,8,384]{2,0,1:T(8,128)(2,1)} %bitcast.73), calls=%async_computation | async-start | bytes 1966080 | tf_op jit(solution)/shard_map/all_to_all | solution.py:41
  152.2 20.3 %all-to-all-start.7 = ((bf16[32,40,384]{2,1,0:T(8,128)(2,1)}), bf16[32,40,384]{2,1,0:T(8,128)(2,1)}, u32[]{:S(2)}, u32[]{:S(2)}) async-start(bf16[32,40,384]{2,1,0:T(8,128)(2,1)} %get-tuple-element.67), calls=%async_computation.7 | async-start | bytes 1966080 | tf_op jit(solution)/shard_map/all_to_all | solution.py:79
  159.2 32.9 %copy-start.1 = (bf16[32,40,384]{2,1,0:T(8,128)(2,1)S(1)}, bf16[32,40,384]{2,1,0:T(8,128)(2,1)}, u32[]{:S(2)}) copy-start(bf16[32,40,384]{2,1,0:T(8,128)(2,1)} %get-tuple-element.68) | copy-start | bytes 2949124
  210.5 39.7 %all-to-all-start.4 = ((bf16[32,40,384]{2,1,0:T(8,128)(2,1)}), bf16[32,40,384]{2,1,0:T(8,128)(2,1)}, u32[]{:S(2)}, u32[]{:S(2)}) async-start(bf16[32,40,384]{2,1,0:T(8,128)(2,1)} %get-tuple-element.70), calls=%async_computation.4 | async-start | bytes 1966080 | tf_op jit(solution)/shard_map/all_to_all | solution.py:72
  247.4 6.5 %copy-start = (bf16[1280,3,128]{2,1,0:T(4,128)(2,1)S(1)}, bf16[1280,3,128]{2,1,0:T(4,128)(2,1)}, u32[]{:S(2)}) copy-start(bf16[1280,3,128]{2,1,0:T(4,128)(2,1)} %concatenate.20) | copy-start | bytes 2949124
  283.7 2.1 copy-start.2
  291.9 2.1 copy-start.2
  300.1 2.1 copy-start.2
  308.3 2.1 copy-start.2
  316.4 2.1 copy-start.2
